TPU v7x, 32 devices: a whole 2x2x4 slice. The times are simulated.
32 devices in a mesh: flow: 4 (over y, core), link: 8 (over z, x).
Axes of the slice: x: 2, y: 2, z: 4, core: 2. Of those that a mesh axis runs over, the one named last changes fastest.
Arguments:
- route_tiles: bfloat16 [512, 1024, 128], P('flow', 'link'), may hold values from 0 to 1, as said below
- tile_count: int32 [4, 8], P('flow', 'link'), may hold values from 16 to 128, as said below
- tile_flow: int32 [4, 1024], P('flow', 'link'), may hold values from 0 to 1023
- tile_link: int32 [4, 1024], P('flow', 'link'), may hold values from 0 to 511, as said below
- flow_class: int32 [524288], P('flow'), may hold values from 0 to 255
- class_weight: float32 [256], replicated, may hold values from 0.25 to 4
- access_price: float32 [524288], P('flow'), may hold values from 0.5 to 4
- capacity: float32 [524288], P('link'), may hold values from 1 to 8
- init_price: float32 [524288], P('link'), may hold values from 0.5 to 2
Outputs:
- flow_rate: float32 [524288], P('flow')
- link_price: float32 [524288], P('link')
Inputs may be any that keep to these rules, and one draw needn't show every extreme that they name: `route_tiles`: entries are 0 or 1. `tile_count`: counts follow 128 divided by 1, 2, 4 or 8; some device uses all 128 slots in every draw. `tile_link`: within one device's slots no link block repeats.
All inputs are finite; a program needn't handle non-finite values.
Results may differ from a plain program's by a relative error of at most 0.0014.
Values may be sent and summed in bfloat16 or wider, within the bound.
A program may use at most 64 MiB of HBM per device.

v0:
```python
import jax
import jax.numpy as jnp
from jax import lax
from jax.sharding import PartitionSpec as P

ITERS = 2


step_size = 0.5


def on_device(
    route_tiles,
    tile_count,
    tile_flow,
    tile_link,
    flow_class,
    class_weight,
    access_price,
    capacity,
    init_price,
):
    slots = route_tiles.shape[0]
    tile = route_tiles.shape[2]
    valid = (jnp.arange(slots, dtype=jnp.int32) < tile_count[0, 0]).astype(jnp.float32)
    flow_idx = tile_flow[0]
    link_idx = tile_link[0]
    flow_blocks = access_price.shape[0] // tile
    link_blocks = capacity.shape[0] // tile
    link_cap = capacity.reshape(link_blocks, tile)
    price = init_price.reshape(link_blocks, tile)
    share_rows = flow_blocks // lax.axis_size("link")
    share_first = lax.axis_index("link") * (share_rows * tile)
    class_piece = lax.dynamic_slice_in_dim(flow_class, share_first, share_rows * tile, 0)
    weight_piece = jnp.take(class_weight, class_piece).reshape(share_rows, tile)
    access_piece = lax.dynamic_slice_in_dim(
        access_price, share_first, share_rows * tile, 0
    ).reshape(share_rows, tile)
    rate_piece = jnp.zeros((1, tile), jnp.float32)
    for step in range(ITERS):
        price_b = price.astype(jnp.bfloat16)
        picked = jnp.take(price_b, link_idx, axis=0)
        term = (
            jnp.einsum("sab,sa->sb", route_tiles, picked, preferred_element_type=jnp.float32)
            * valid[:, None]
        )
        route_part = jax.ops.segment_sum(term, flow_idx, num_segments=flow_blocks)
        route_piece = lax.psum_scatter(route_part, "link", scatter_dimension=0, tiled=True)
        rate_piece = weight_piece / (access_piece + route_piece)
        rate_b = lax.all_gather(rate_piece.astype(jnp.bfloat16), "link", axis=0, tiled=True)
        sent = jnp.take(rate_b, flow_idx, axis=0)
        term = (
            jnp.einsum("sab,sb->sa", route_tiles, sent, preferred_element_type=jnp.float32)
            * valid[:, None]
        )
        load_part = jax.ops.segment_sum(term, link_idx, num_segments=link_blocks)
        load = lax.psum(load_part, "flow")
        price = price * jnp.exp(step_size * (load / link_cap - 1.0))
    rate = lax.all_gather(rate_piece, "link", axis=0, tiled=True)
    return (rate.reshape(-1), price.reshape(-1))


def solution(mesh):
    return jax.shard_map(
        on_device,
        mesh=mesh,
        in_specs=(
            P("flow", "link", None),
            P("flow", "link"),
            P("flow", "link"),
            P("flow", "link"),
            P("flow"),
            P(),
            P("flow"),
            P("link"),
            P("link"),
        ),
        out_specs=(P("flow"), P("link")),
        check_vma=False,
    )
```

profile of v0, /device:TPU:0, one launch (start us, length us, event | category | flops | bytes accessed | tf_op | source)
XLA Modules:
  0.0 341.7 jit_solution(13563582530019606276)
XLA Ops:
  9.2 1.0 bitcast_convert_fusion
  10.2 0.7 gather_fusion.1
  11.0 3.4 fusion.26
  14.4 1.9 scatter_custom_fusion
  16.3 0.9 fusion.32
  17.2 101.9 %gather_fusion = f32[16384]{0:T(1024)S(1)} fusion(f32[256]{0:T(256)S(1)} %copy-done, s32[16384]{0:T(1024)S(1)} %fusion.32), kind=kCustom, calls=%fused_computation.4 | custom fusion | bytes 196608 | tf_op jit(solution)/shard_map/jit(_take)/gather | solution.py:35
  119.2 1.0 fusion.18
  120.2 32.5 %all_gather.9 = bf16[1024,128]{1,0:T(8,128)(2,1)S(1)} all-gather(bf16[128,128]{1,0:T(8,128)(2,1)S(1)} %fusion.18), channel_id=1, replica_groups=mesh['flow'=4,'link'=8] {'link'}, dimensions={0}, use_global_device_ids=true | all-gather | bytes 294912 | tf_op jit(solution)/shard_map/all_gather | solution.py:50
  152.7 0.7 gather_fusion.2
  153.5 4.4 %fusion.24 = f32[128,1,128]{2,1,0:T(1,128)S(1)} fusion(bf16[128,128,128]{2,1,0:T(8,128)(2,1)} %param.13, bf16[128,128,1]{1,0,2:T(8,128)(2,1)S(1)} %select_bitcast_fusion.2), kind=kOutput, calls=%fused_computation.39 | convolution fusion | flops 4194304 | bytes 4292608 | tf_op jit(solution)/shard_map/sab,sb->sa/dot_general | solution.py:53
  157.9 1.9 scatter_custom_fusion.1
  159.9 33.0 %all-reduce.3.cloned.1.call-done = f32[512,128]{1,0:T(8,128)} async-done(((f32[512,128]{1,0:T(8,128)}), f32[512,128]{1,0:T(8,128)}) %all-reduce.3.cloned.1.call-update) | async-done | bytes 262160 | tf_op jit(solution)/shard_map/psum | solution.py:57
  193.0 1.0 fusion.37
  194.0 0.7 gather_fusion.3
  194.8 3.4 fusion.22
  198.2 1.9 scatter_custom_fusion.2
  200.1 62.0 %reduce-scatter.5.cloned.1.call-done = f32[128,128]{1,0:T(8,128)} async-done(((f32[1024,128]{1,0:T(8,128)}), f32[128,128]{1,0:T(8,128)}) %reduce-scatter.5.cloned.1.call-update) | async-done | bytes 65552 | tf_op jit(solution)/shard_map/reduce_scatter | solution.py:48
  262.2 0.9 fusion.38
  263.1 30.9 %all_gather.11 = bf16[1024,128]{1,0:T(8,128)(2,1)S(1)} all-gather(bf16[128,128]{1,0:T(8,128)(2,1)S(1)} %get-tuple-element.4), channel_id=1, replica_groups=mesh['flow'=4,'link'=8] {'link'}, dimensions={0}, use_global_device_ids=true | all-gather | bytes 294912 | tf_op jit(solution)/shard_map/all_gather | solution.py:50
  294.8 4.5 %fusion.20 = f32[128,1,128]{2,1,0:T(1,128)S(1)} fusion(bf16[128,128,128]{2,1,0:T(8,128)(2,1)} %param.13, bf16[128,128,1]{1,0,2:T(8,128)(2,1)S(1)} %select_bitcast_fusion), kind=kOutput, calls=%fused_computation.35 | convolution fusion | flops 4194304 | bytes 4292608 | tf_op jit(solution)/shard_map/sab,sb->sa/dot_general | solution.py:53
  299.2 1.9 scatter_custom_fusion.3
  301.1 31.4 %all_gather.10 = f32[1024,128]{1,0:T(8,128)S(1)} all-gather(f32[128,128]{1,0:T(8,128)S(1)} %get-tuple-element.5), channel_id=1, replica_groups=mesh['flow'=4,'link'=8] {'link'}, dimensions={0}, use_global_device_ids=true | all-gather | bytes 589824 | tf_op jit(solution)/shard_map/all_gather | solution.py:59
  332.6 1.8 fusion.8
  334.4 0.8 copy.31
  (32 shorter events, 2.7 us)
Async XLA Ops:
  7.2 10.0 %copy-start = (f32[256]{0:T(256)S(1)}, f32[256]{0:T(256)}, u32[]{:S(2)}) copy-start(f32[256]{0:T(256)} %param.18) | copy-start | bytes 3076
  7.2 7.2 %copy-start.4 = (s32[1,128]{1,0:T(1,128)S(1)}, s32[1,128]{1,0:T(1,128)}, u32[]{:S(2)}) copy-start(s32[1,128]{1,0:T(1,128)} %param.15) | copy-start | bytes 1540
  7.2 112.0 %reduce-scatter.3.cloned.1.call-start = ((), (), s32[]{:S(2)}) async-start(), calls=%async_computation.2 | async-start | bytes 589824 | tf_op jit(solution)/shard_map/reduce_scatter | solution.py:48
  16.3 176.7 %all-reduce.3.cloned.1.call-start = ((), (), s32[]{:S(2)}) async-start(), calls=%async_computation.3 | async-start | bytes 524288 | tf_op jit(solution)/shard_map/psum | solution.py:57
  119.1 73.9 %copy-start.1 = (f32[65536]{0:T(1024)S(1)}, f32[65536]{0:T(1024)}, u32[]{:S(2)}) copy-start(f32[65536]{0:T(1024)} %param.21) | copy-start | bytes 786436
  119.1 73.9 %copy-start.2 = (f32[65536]{0:T(1024)S(1)}, f32[65536]{0:T(1024)}, u32[]{:S(2)}) copy-start(f32[65536]{0:T(1024)} %param.20) | copy-start | bytes 786436
  159.9 102.3 %reduce-scatter.5.cloned.1.call-start = ((), (), s32[]{:S(2)}) async-start(), calls=%async_computation.4 | async-start | bytes 589824 | tf_op jit(solution)/shard_map/reduce_scatter | solution.py:48
  198.2 134.4 %copy-start.3 = (f32[512,128]{1,0:T(8,128)S(1)}, f32[512,128]{1,0:T(8,128)}, u32[]{:S(2)}) copy-start(f32[512,128]{1,0:T(8,128)} %all-reduce.3.cloned.1.call-done) | copy-start | bytes 786436
  200.1 132.5 %all-reduce.5.cloned.1.call-start = ((), (), s32[]{:S(2)}) async-start(), calls=%async_computation.5 | async-start | bytes 524288 | tf_op jit(solution)/shard_map/psum | solution.py:57
Sparse Core Ops, SparseCore 0:
  16.4 65.2 reduce-scatter.2
  160.0 32.9 all-reduce.2
  200.2 61.9 reduce-scatter.4
  301.3 31.0 all-reduce.4
where the time goes:
time: 342 us
  local copies, waits for them, and re-layouts  106 us (31%)
  waiting for transfers between devices  95.1 us (28%)
  blocking collectives  94.8 us (28%)
  other arithmetic  15.8 us (5%)
  matrix products  15.6 us (5%)
  between operations  14.6 us (4%)
    gather x1, local copies, waits for them, and re-layouts, on_device(): weight_piece = jnp.take(class_weight, class_piece).reshape(share_rows, tile)  102 us
    all_gather x2, blocking collectives, on_device(): lax.all_gather(rate_piece.astype(jnp.bfloat16), 'link', axis=0, tiled=True)  63.4 us
    reduce_scatter x2, waiting for transfers between devices, on_device(): lax.psum_scatter(route_part, 'link', scatter_dimension=0, tiled=True)  62 us
    psum x2, waiting for transfers between devices, on_device(): load = lax.psum(load_part, 'flow')  33 us
    all_gather x1, blocking collectives, on_device(): rate = lax.all_gather(rate_piece, 'link', axis=0, tiled=True)  31.4 us
    dot_general x2, matrix products, on_device(): jnp.einsum('sab,sb->sa', route_tiles, sent, preferred_element_type=jnp.fl...  8.89 us
  transfers between devices with their start and end apart: 4, of which 2 were waited for; matrix products, arithmetic and copies ran while one was open for 30% of the time, Pallas kernels for 0%

commit v1 on v0

v1 whole, which is shorter than its diff:
```python
import functools

import jax
import jax.numpy as jnp
from jax import lax
from jax.experimental import pallas as pl
from jax.experimental.pallas import tpu as pltpu
from jax.sharding import PartitionSpec as P

ITERS = 2
STEP = 0.5
GROUP = 16
F32, BF16 = jnp.float32, jnp.bfloat16


def iota(shape, dim):
    return lax.broadcasted_iota(jnp.int32, shape, dim)


def halves(x):
    high = x.astype(BF16)
    low = (x - high.astype(F32)).astype(BF16)
    return high, low


def kernel(
    n_flow, n_link,
    tiles_hbm, count_ref, flow_smem, flow_ref, link_ref, class_ref, table_ref, access_ref, cap_ref, price_ref,
    rate_out, price_out,
    tiles, flow_all, link_all, route_buf, load_buf, picked, term, rate_b, match, parts, own_class, own_access, price,
    tile_sem, idx_send, flow_recv, link_recv, route_send, route_recv, load_send, load_recv,
):
    slots, size = tiles.shape[0], tiles.shape[1]
    link_blocks, flow_blocks = price_ref.shape[0], access_ref.shape[0]
    me_f, me_l = lax.axis_index("flow"), lax.axis_index("link")
    barrier = pltpu.get_barrier_semaphore()
    link_peers = [lax.rem(me_l + k, n_link) for k in range(1, n_link)]
    flow_peers = [lax.rem(me_f + k, n_flow) for k in range(1, n_flow)]
    for peer in link_peers:
        pl.semaphore_signal(barrier, inc=1, device_id={"link": peer})
    for peer in flow_peers:
        pl.semaphore_signal(barrier, inc=1, device_id={"flow": peer})

    chunk = slots // tile_sem.shape[0]
    loads = []
    for c in range(tile_sem.shape[0]):
        copy = pltpu.make_async_copy(
            tiles_hbm.at[pl.ds(c * chunk, chunk)], tiles.at[pl.ds(c * chunk, chunk)], tile_sem.at[c]
        )
        copy.start()
        loads.append(copy)

    count = count_ref[0, 0]
    used = iota((8, slots), 1) < count
    flow_all[me_l] = jnp.where(used, jnp.broadcast_to(flow_ref[...], (8, slots)), -1)
    link_all[me_f] = jnp.where(used, jnp.broadcast_to(link_ref[...], (8, slots)), -1)
    pl.semaphore_wait(barrier, n_link + n_flow - 2)

    def to_link(buf, send, recv):
        return [
            pltpu.make_async_remote_copy(
                src_ref=buf.at[me_l], dst_ref=buf.at[me_l], send_sem=send.at[k], recv_sem=recv.at[me_l],
                device_id={"link": peer}, device_id_type=pl.DeviceIdType.MESH,
            )
            for k, peer in enumerate(link_peers)
        ]

    def to_flow(buf, send, recv):
        return [
            pltpu.make_async_remote_copy(
                src_ref=buf.at[me_f], dst_ref=buf.at[me_f], send_sem=send.at[k], recv_sem=recv.at[me_f],
                device_id={"flow": peer}, device_id_type=pl.DeviceIdType.MESH,
            )
            for k, peer in enumerate(flow_peers)
        ]

    def arrived(buf, send, recv, k, source, axis):
        pltpu.make_async_remote_copy(
            src_ref=buf.at[source], dst_ref=buf.at[source], send_sem=send.at[k], recv_sem=recv.at[source],
            device_id={axis: source}, device_id_type=pl.DeviceIdType.MESH,
        ).wait_recv()

    link_sources = [lax.rem(me_l + n_link - k, n_link) for k in range(1, n_link)]
    flow_sources = [lax.rem(me_f + n_flow - k, n_flow) for k in range(1, n_flow)]
    pending = to_link(flow_all, idx_send.at[0], flow_recv) + to_flow(link_all, idx_send.at[1], link_recv)
    for copy in pending:
        copy.start()

    def column(row):
        return jnp.broadcast_to(row.astype(F32), (slots, slots)).T

    lane = iota((slots, slots), 1)
    link_col = column(link_ref[...])
    pick = jnp.concatenate(
        [(link_col == (lane + k * slots).astype(F32)).astype(BF16) for k in range(link_blocks // slots)], axis=1
    )
    row_used = iota((slots, size), 0) < count
    group_row = iota((GROUP, size), 0)

    def route_terms(first):
        def body(g, carry):
            at = pl.multiple_of(g * GROUP, GROUP)
            p = picked[pl.ds(at, GROUP), :]
            left = jnp.concatenate(
                [jnp.where(group_row == k, p, jnp.zeros_like(p)).astype(BF16) for k in range(GROUP)], axis=1
            )
            right = tiles[pl.ds(at, GROUP)].reshape(GROUP * size, size)
            term[pl.ds(at, GROUP), :] = jnp.dot(left, right, preferred_element_type=F32)
            return carry

        if first:
            per = chunk // GROUP
            for c, copy in enumerate(loads):
                copy.wait()
                lax.fori_loop(c * per, (c + 1) * per, body, 0)
        else:
            lax.fori_loop(0, slots // GROUP, body, 0)

    def load_terms():
        def body(g, carry):
            at = pl.multiple_of(g * GROUP, GROUP)
            q = rate_b[pl.ds(at, GROUP), :]
            right = tiles[pl.ds(at, GROUP)].reshape(GROUP * size, size)
            full = lax.dot_general(q, right, (((1,), (1,)), ((), ())), preferred_element_type=F32)
            total = jnp.zeros((GROUP, size), F32)
            for k in range(GROUP):
                total = jnp.where(group_row == k, full[:, k * size : (k + 1) * size], total)
            term[pl.ds(at, GROUP), :] = total
            return carry

        lax.fori_loop(0, slots // GROUP, body, 0)

    def weights(classes):
        out = jnp.zeros(classes.shape, F32)
        low, high = classes % size, classes // size
        for k in range(table_ref.shape[0]):
            table = jnp.broadcast_to(table_ref[k : k + 1, :], classes.shape)
            out = jnp.where(high == k, jnp.take_along_axis(table, low, axis=1), out)
        return out

    price[...] = price_ref[...]
    for it in range(ITERS):
        picked[...] = jnp.dot(pick, price[...].astype(BF16), preferred_element_type=F32)
        route_terms(it == 0)
        route_buf[it, me_l] = jnp.where(row_used, term[...], 0.0)
        sends = to_link(route_buf.at[it], route_send.at[it], route_recv.at[it])
        for copy in sends:
            copy.start()
        pending += sends
        if it == 0:
            def own(s, carry):
                f = flow_smem[0, s]
                own_class[pl.ds(s, 1), :] = class_ref[pl.ds(f, 1), :]
                own_access[pl.ds(s, 1), :] = access_ref[pl.ds(f, 1), :]
                return carry

            lax.fori_loop(0, slots, own, 0, unroll=8)
            own_weight = weights(own_class[...])
            for k, source in enumerate(link_sources):
                arrived(flow_all, idx_send.at[0], flow_recv, k, source, "link")
            flow_col = column(flow_ref[...])
            for d in range(n_link):
                same = (flow_col == flow_all[d, 0:1, :].astype(F32)).astype(BF16)
                match[d, :, :slots] = same
                match[d, :, slots:] = same

        route = jnp.zeros((slots, size), F32)
        for k, source in enumerate([me_l] + link_sources):
            if k:
                arrived(route_buf.at[it], route_send.at[it], route_recv.at[it], k - 1, source, "link")
            high, low = halves(route_buf[it, source])
            both = jnp.concatenate([high, low], axis=0)
            if it == ITERS - 1:
                parts[source] = both
            route = route + jnp.dot(match[source], both, preferred_element_type=F32)
        rate_b[...] = (own_weight / (own_access[...] + route)).astype(BF16)
        load_terms()
        load_buf[it, me_f] = jnp.where(row_used, term[...], 0.0)
        sends = to_flow(load_buf.at[it], load_send.at[it], load_recv.at[it])
        for copy in sends:
            copy.start()
        pending += sends
        if it == 0:
            for k, source in enumerate(flow_sources):
                arrived(link_all, idx_send.at[1], link_recv, k, source, "flow")
        if it == ITERS - 1:
            def rows(r, carry):
                at = pl.multiple_of(r * size, size)
                number = iota((size, slots), 0) + at
                route = jnp.zeros((size, size), F32)
                for d in range(n_link):
                    same = (number == flow_all[d, 0:1, :]).astype(F32).astype(BF16)
                    route = route + jnp.dot(
                        jnp.concatenate([same, same], axis=1), parts[d], preferred_element_type=F32
                    )
                block = pl.ds(at, size)
                rate_out[block, :] = weights(class_ref[block, :]) / (access_ref[block, :] + route)
                return carry

            lax.fori_loop(0, flow_blocks // size, rows, 0)

        load = jnp.zeros((link_blocks, size), F32)
        block_row = iota((link_blocks, slots), 0)
        for k, source in enumerate([me_f] + flow_sources):
            if k:
                arrived(load_buf.at[it], load_send.at[it], load_recv.at[it], k - 1, source, "flow")
            high, low = halves(load_buf[it, source])
            same = (block_row == link_all[source, 0:1, :]).astype(F32).astype(BF16)
            load = load + jnp.dot(
                jnp.concatenate([same, same], axis=1),
                jnp.concatenate([high, low], axis=0),
                preferred_element_type=F32,
            )
        new = price[...] * jnp.exp(STEP * (load / cap_ref[...] - 1.0))
        if it == ITERS - 1:
            price_out[...] = new
        else:
            price[...] = new
    for copy in pending:
        copy.wait_send()


def on_device(n_flow, n_link, route_tiles, tile_count, tile_flow, tile_link, flow_class, class_weight, access_price,
              capacity, init_price):
    slots, _, size = route_tiles.shape
    flow_blocks, link_blocks = access_price.shape[0] // size, capacity.shape[0] // size
    vmem = pl.BlockSpec(memory_space=pltpu.VMEM)
    smem = pl.BlockSpec(memory_space=pltpu.SMEM)
    dma = pltpu.SemaphoreType.DMA
    peers = max(n_flow, n_link)
    rate, price = pl.pallas_call(
        functools.partial(kernel, n_flow, n_link),
        out_shape=(
            jax.ShapeDtypeStruct((flow_blocks, size), F32),
            jax.ShapeDtypeStruct((link_blocks, size), F32),
        ),
        in_specs=[pl.BlockSpec(memory_space=pl.ANY), smem, smem] + [vmem] * 7,
        out_specs=(vmem, vmem),
        scratch_shapes=[
            pltpu.VMEM((slots, size, size), BF16),
            pltpu.VMEM((n_link, 8, slots), jnp.int32),
            pltpu.VMEM((n_flow, 8, slots), jnp.int32),
            pltpu.VMEM((ITERS, n_link, slots, size), F32),
            pltpu.VMEM((ITERS, n_flow, slots, size), F32),
            pltpu.VMEM((slots, size), F32),
            pltpu.VMEM((slots, size), F32),
            pltpu.VMEM((slots, size), BF16),
            pltpu.VMEM((n_link, slots, 2 * slots), BF16),
            pltpu.VMEM((n_link, 2 * slots, size), BF16),
            pltpu.VMEM((slots, size), jnp.int32),
            pltpu.VMEM((slots, size), F32),
            pltpu.VMEM((link_blocks, size), F32),
            dma((4,)),
            dma((2, peers)),
            dma((n_link,)),
            dma((n_flow,)),
            dma((ITERS, n_link)),
            dma((ITERS, n_link)),
            dma((ITERS, n_flow)),
            dma((ITERS, n_flow)),
        ],
        compiler_params=pltpu.CompilerParams(
            collective_id=0, has_side_effects=True, vmem_limit_bytes=48 * 1024 * 1024
        ),
    )(
        route_tiles, tile_count, tile_flow, tile_flow, tile_link,
        flow_class.reshape(flow_blocks, size), class_weight.reshape(-1, size),
        access_price.reshape(flow_blocks, size), capacity.reshape(link_blocks, size),
        init_price.reshape(link_blocks, size),
    )
    return rate.reshape(-1), price.reshape(-1)


def solution(mesh):
    return jax.shard_map(
        functools.partial(on_device, mesh.shape["flow"], mesh.shape["link"]),
        mesh=mesh,
        in_specs=(
            P("flow", "link", None),
            P("flow", "link"),
            P("flow", "link"),
            P("flow", "link"),
            P("flow"),
            P(),
            P("flow"),
            P("link"),
            P("link"),
        ),
        out_specs=(P("flow"), P("link")),
        check_vma=False,
    )
```

time: 342 us -> 56.8 us (0.17)
  the two profiles are of different devices: /device:TPU:0 before, /device:TPU:31 now
where the time goes in v1:
time: 56.8 us; the launch traced here: 56.5 us
  Pallas kernels  47.7 us (84%)
  local copies, waits for them, and re-layouts  7.51 us (13%)
  between operations  1.3 us (2%)
    pallas_call x1, Pallas kernels, on_device(): pl.pallas_call(functools.partial(kernel, n_flow, n_link), out_shape=(jax....  47.7 us
    unnamed x16, local copies, waits for them, and re-layouts  7.51 us

profile of v1, /device:TPU:31, one launch (start us, length us, event | category | flops | bytes accessed | tf_op | source)
XLA Modules:
  0.0 56.5 jit_solution(8276137587489174346)
XLA Ops:
  1.3 0.0 copy-start
  1.3 1.0 %copy-done = s32[131072]{0:T(1024)S(1)} copy-done((s32[131072]{0:T(1024)S(1)}, s32[131072]{0:T(1024)}, u32[]{:S(2)}) %copy-start) | copy-done | bytes 524312
  2.3 0.0 copy-start.1
  2.3 1.0 %copy-done.1 = f32[131072]{0:T(1024)S(1)} copy-done((f32[131072]{0:T(1024)S(1)}, f32[131072]{0:T(1024)}, u32[]{:S(2)}) %copy-start.1) | copy-done | bytes 524312
  3.4 0.0 copy-start.2
  3.4 0.9 %copy-done.2 = f32[65536]{0:T(1024)S(1)} copy-done((f32[65536]{0:T(1024)S(1)}, f32[65536]{0:T(1024)}, u32[]{:S(2)}) %copy-start.2) | copy-done | bytes 262168
  4.3 0.0 copy-start.3
  4.3 0.9 %copy-done.3 = f32[65536]{0:T(1024)S(1)} copy-done((f32[65536]{0:T(1024)S(1)}, f32[65536]{0:T(1024)}, u32[]{:S(2)}) %copy-start.3) | copy-done | bytes 262168
  5.3 0.0 copy-start.4
  5.3 0.7 %copy-done.4 = s32[1,128]{1,0:T(1,128)S(1)} copy-done((s32[1,128]{1,0:T(1,128)S(1)}, s32[1,128]{1,0:T(1,128)}, u32[]{:S(2)}) %copy-start.4) | copy-done | bytes 536
  5.9 0.0 copy-start.5
  5.9 0.7 %copy-done.5 = f32[256]{0:T(256)S(1)} copy-done((f32[256]{0:T(256)S(1)}, f32[256]{0:T(256)}, u32[]{:S(2)}) %copy-start.5) | copy-done | bytes 1048
  6.6 0.0 copy-start.6
  6.6 0.7 %copy-done.6 = s32[1,128]{1,0:T(1,128)S(1)} copy-done((s32[1,128]{1,0:T(1,128)S(1)}, s32[1,128]{1,0:T(1,128)}, u32[]{:S(2)}) %copy-start.6) | copy-done | bytes 536
  7.3 47.7 %shard_map.104 = (f32[1024,128]{1,0:T(8,128)S(1)}, f32[512,128]{1,0:T(8,128)S(1)}) custom-call(bf16[128,128,128]{2,1,0:T(8,128)(2,1)} %tiles_hbm.1, s32[1,1]{1,0:T(1,128)S(6)} %copy.13.count_ref, s32[1,128]{1,0:T(1,128)S(1)} %copy-done.4, s32[1,128]{1,0:T(1,128)S(1)} %copy-done.4, s32[1,128]{1,0:T(1,128)S(1)} %copy-done.6, s32[1024,128]{1,0:T(8,128)S(1)} %bitcast.7, ...), custom_call_target="tpu_custom_call" | custom-call | tf_op jit(solution)/shard_map/pallas_call | solution.py:231
  55.0 0.8 %copy.14 = f32[131072]{0:T(1024)} copy(f32[131072]{0:T(1024)S(1)} %bitcast.9) | data formatting | bytes 1048576
  55.8 0.7 %copy.15 = f32[65536]{0:T(1024)} copy(f32[65536]{0:T(1024)S(1)} %bitcast.12) | data formatting | bytes 524288
Async XLA Ops:
  1.3 1.0 %copy-start = (s32[131072]{0:T(1024)S(1)}, s32[131072]{0:T(1024)}, u32[]{:S(2)}) copy-start(s32[131072]{0:T(1024)} %param.13) | copy-start | bytes 1572868
  2.3 1.0 %copy-start.1 = (f32[131072]{0:T(1024)S(1)}, f32[131072]{0:T(1024)}, u32[]{:S(2)}) copy-start(f32[131072]{0:T(1024)} %param.15) | copy-start | bytes 1572868
  3.4 0.9 %copy-start.2 = (f32[65536]{0:T(1024)S(1)}, f32[65536]{0:T(1024)}, u32[]{:S(2)}) copy-start(f32[65536]{0:T(1024)} %param.16) | copy-start | bytes 786436
  4.3 0.9 %copy-start.3 = (f32[65536]{0:T(1024)S(1)}, f32[65536]{0:T(1024)}, u32[]{:S(2)}) copy-start(f32[65536]{0:T(1024)} %param.17) | copy-start | bytes 786436
  5.3 0.7 %copy-start.4 = (s32[1,128]{1,0:T(1,128)S(1)}, s32[1,128]{1,0:T(1,128)}, u32[]{:S(2)}) copy-start(s32[1,128]{1,0:T(1,128)} %flow_ref.1) | copy-start | bytes 1540
  5.9 0.7 %copy-start.5 = (f32[256]{0:T(256)S(1)}, f32[256]{0:T(256)}, u32[]{:S(2)}) copy-start(f32[256]{0:T(256)} %param.14) | copy-start | bytes 3076
  6.6 0.7 %copy-start.6 = (s32[1,128]{1,0:T(1,128)S(1)}, s32[1,128]{1,0:T(1,128)}, u32[]{:S(2)}) copy-start(s32[1,128]{1,0:T(1,128)} %link_ref.1) | copy-start | bytes 1540

commit v2 on v1

--- a/solution.py
+++ b/solution.py
@@ -25,13 +25,14 @@
 
 def kernel(
     n_flow, n_link,
-    tiles_hbm, count_ref, flow_smem, flow_ref, link_ref, class_ref, table_ref, access_ref, cap_ref, price_ref,
+    tiles_hbm, count_ref, flow_smem, flow_hbm, link_hbm, class_hbm, table_hbm, access_hbm, cap_hbm, price_hbm,
     rate_out, price_out,
     tiles, flow_all, link_all, route_buf, load_buf, picked, term, rate_b, match, parts, own_class, own_access, price,
-    tile_sem, idx_send, flow_recv, link_recv, route_send, route_recv, load_send, load_recv,
+    flow_ref, link_ref, class_ref, table_ref, access_ref, cap_ref,
+    tile_sem, in_sem, idx_send, flow_recv, link_recv, route_send, route_recv, load_send, load_recv,
 ):
     slots, size = tiles.shape[0], tiles.shape[1]
-    link_blocks, flow_blocks = price_ref.shape[0], access_ref.shape[0]
+    link_blocks, flow_blocks = price.shape[0], access_ref.shape[0]
     me_f, me_l = lax.axis_index("flow"), lax.axis_index("link")
     barrier = pltpu.get_barrier_semaphore()
     link_peers = [lax.rem(me_l + k, n_link) for k in range(1, n_link)]
@@ -41,6 +42,15 @@
     for peer in flow_peers:
         pl.semaphore_signal(barrier, inc=1, device_id={"flow": peer})
 
+    inputs = [
+        pltpu.make_async_copy(source, target, in_sem.at[k])
+        for k, (source, target) in enumerate(
+            [(flow_hbm, flow_ref), (link_hbm, link_ref), (price_hbm, price), (class_hbm, class_ref),
+             (access_hbm, access_ref), (table_hbm, table_ref), (cap_hbm, cap_ref)]
+        )
+    ]
+    for copy in inputs[:3]:
+        copy.start()
     chunk = slots // tile_sem.shape[0]
     loads = []
     for c in range(tile_sem.shape[0]):
@@ -50,6 +60,10 @@
         copy.start()
         loads.append(copy)
 
+    for copy in inputs[3:]:
+        copy.start()
+    for copy in inputs[:2]:
+        copy.wait()
     count = count_ref[0, 0]
     used = iota((8, slots), 1) < count
     flow_all[me_l] = jnp.where(used, jnp.broadcast_to(flow_ref[...], (8, slots)), -1)
@@ -130,6 +144,19 @@
 
         lax.fori_loop(0, slots // GROUP, body, 0)
 
+    def encode(buf, it, slot):
+        x = jnp.where(row_used, term[...], 0.0)
+        level = jnp.ceil(jnp.log2(jnp.maximum(jnp.max(x, axis=0, keepdims=True), 1e-30)) * 8.0)
+        y = jnp.sqrt(x * jnp.exp2(level * -0.125)) * 65535.0 - 32768.0
+        code = jnp.clip(jnp.round(y), -32768.0, 32767.0).astype(jnp.int32)
+        buf[it, slot, :slots, :] = code.astype(jnp.int16)
+        buf[it, slot, slots:, :] = jnp.broadcast_to(level.astype(jnp.int32), (GROUP, size)).astype(jnp.int16)
+
+    def decode(buf, it, slot):
+        y = (buf[it, slot, :slots, :].astype(jnp.int32).astype(F32) + 32768.0) * (1.0 / 65535.0)
+        level = buf[it, slot, slots:, :].astype(jnp.int32).astype(F32)[:1, :]
+        return y * y * jnp.exp2(level * 0.125)
+
     def weights(classes):
         out = jnp.zeros(classes.shape, F32)
         low, high = classes % size, classes // size
@@ -138,16 +165,19 @@
             out = jnp.where(high == k, jnp.take_along_axis(table, low, axis=1), out)
         return out
 
-    price[...] = price_ref[...]
+    inputs[2].wait()
     for it in range(ITERS):
         picked[...] = jnp.dot(pick, price[...].astype(BF16), preferred_element_type=F32)
         route_terms(it == 0)
-        route_buf[it, me_l] = jnp.where(row_used, term[...], 0.0)
+        encode(route_buf, it, me_l)
         sends = to_link(route_buf.at[it], route_send.at[it], route_recv.at[it])
         for copy in sends:
             copy.start()
         pending += sends
         if it == 0:
+            for copy in inputs[3:]:
+                copy.wait()
+
             def own(s, carry):
                 f = flow_smem[0, s]
                 own_class[pl.ds(s, 1), :] = class_ref[pl.ds(f, 1), :]
@@ -168,14 +198,14 @@
         for k, source in enumerate([me_l] + link_sources):
             if k:
                 arrived(route_buf.at[it], route_send.at[it], route_recv.at[it], k - 1, source, "link")
-            high, low = halves(route_buf[it, source])
+            high, low = halves(decode(route_buf, it, source))
             both = jnp.concatenate([high, low], axis=0)
             if it == ITERS - 1:
                 parts[source] = both
             route = route + jnp.dot(match[source], both, preferred_element_type=F32)
         rate_b[...] = (own_weight / (own_access[...] + route)).astype(BF16)
         load_terms()
-        load_buf[it, me_f] = jnp.where(row_used, term[...], 0.0)
+        encode(load_buf, it, me_f)
         sends = to_flow(load_buf.at[it], load_send.at[it], load_recv.at[it])
         for copy in sends:
             copy.start()
@@ -204,7 +234,7 @@
         for k, source in enumerate([me_f] + flow_sources):
             if k:
                 arrived(load_buf.at[it], load_send.at[it], load_recv.at[it], k - 1, source, "flow")
-            high, low = halves(load_buf[it, source])
+            high, low = halves(decode(load_buf, it, source))
             same = (block_row == link_all[source, 0:1, :]).astype(F32).astype(BF16)
             load = load + jnp.dot(
                 jnp.concatenate([same, same], axis=1),
@@ -225,6 +255,7 @@
     slots, _, size = route_tiles.shape
     flow_blocks, link_blocks = access_price.shape[0] // size, capacity.shape[0] // size
     vmem = pl.BlockSpec(memory_space=pltpu.VMEM)
+    hbm = pl.BlockSpec(memory_space=pltpu.HBM)
     smem = pl.BlockSpec(memory_space=pltpu.SMEM)
     dma = pltpu.SemaphoreType.DMA
     peers = max(n_flow, n_link)
@@ -234,14 +265,14 @@
             jax.ShapeDtypeStruct((flow_blocks, size), F32),
             jax.ShapeDtypeStruct((link_blocks, size), F32),
         ),
-        in_specs=[pl.BlockSpec(memory_space=pl.ANY), smem, smem] + [vmem] * 7,
+        in_specs=[hbm, smem, smem] + [hbm] * 7,
         out_specs=(vmem, vmem),
         scratch_shapes=[
             pltpu.VMEM((slots, size, size), BF16),
             pltpu.VMEM((n_link, 8, slots), jnp.int32),
             pltpu.VMEM((n_flow, 8, slots), jnp.int32),
-            pltpu.VMEM((ITERS, n_link, slots, size), F32),
-            pltpu.VMEM((ITERS, n_flow, slots, size), F32),
+            pltpu.VMEM((ITERS, n_link, slots + GROUP, size), jnp.int16),
+            pltpu.VMEM((ITERS, n_flow, slots + GROUP, size), jnp.int16),
             pltpu.VMEM((slots, size), F32),
             pltpu.VMEM((slots, size), F32),
             pltpu.VMEM((slots, size), BF16),
@@ -250,7 +281,14 @@
             pltpu.VMEM((slots, size), jnp.int32),
             pltpu.VMEM((slots, size), F32),
             pltpu.VMEM((link_blocks, size), F32),
+            pltpu.VMEM((1, slots), jnp.int32),
+            pltpu.VMEM((1, slots), jnp.int32),
+            pltpu.VMEM((flow_blocks, size), jnp.int32),
+            pltpu.VMEM((class_weight.shape[0] // size, size), F32),
+            pltpu.VMEM((flow_blocks, size), F32),
+            pltpu.VMEM((link_blocks, size), F32),
             dma((4,)),
+            dma((7,)),
             dma((2, peers)),
             dma((n_link,)),
             dma((n_flow,)),
@@ -260,7 +298,7 @@
             dma((ITERS, n_flow)),
         ],
         compiler_params=pltpu.CompilerParams(
-            collective_id=0, has_side_effects=True, vmem_limit_bytes=48 * 1024 * 1024
+            collective_id=0, has_side_effects=True, vmem_limit_bytes=60 * 1024 * 1024
         ),
     )(
         route_tiles, tile_count, tile_flow, tile_flow, tile_link,

time: 56.8 us -> 44.5 us (0.78)
  the two profiles are of different devices: /device:TPU:31 before, /device:TPU:0 now
where the time goes in v2:
time: 44.5 us; the launch traced here: 44.3 us
  Pallas kernels  39.5 us (89%)
  local copies, waits for them, and re-layouts  3.54 us (8%)
  between operations  1.29 us (3%)
    pallas_call x1, Pallas kernels, on_device(): pl.pallas_call(functools.partial(kernel, n_flow, n_link), out_shape=(jax....  39.5 us
    unnamed x2, local copies, waits for them, and re-layouts  3.54 us

profile of v2, /device:TPU:0, one launch (start us, length us, event | category | flops | bytes accessed | tf_op | source)
XLA Modules:
  0.0 44.3 jit_solution(2368667274243714752)
XLA Ops:
  1.3 39.5 %shard_map.104 = (f32[1024,128]{1,0:T(8,128)}, f32[512,128]{1,0:T(8,128)}) custom-call(bf16[128,128,128]{2,1,0:T(8,128)(2,1)} %tiles_hbm.1, s32[1,1]{1,0:T(1,128)S(6)} %copy.13.count_ref, s32[1,128]{1,0:T(1,128)} %flow_hbm.1, s32[1,128]{1,0:T(1,128)} %flow_hbm.1, s32[1,128]{1,0:T(1,128)} %link_hbm.1, s32[1024,128]{1,0:T(8,128)} %bitcast.7, ...), custom_call_target="tpu_custom_call" | custom-call | tf_op jit(solution)/shard_map/pallas_call | solution.py:262
  40.7 1.9 %copy.14 = f32[131072]{0:T(1024)} copy(f32[131072]{0:T(1024)} %bitcast.9) | data formatting | bytes 1048576
  42.6 1.7 %copy.15 = f32[65536]{0:T(1024)} copy(f32[65536]{0:T(1024)} %bitcast.12) | data formatting | bytes 524288

commit v3 on v2

--- a/solution.py
+++ b/solution.py
@@ -10,6 +10,7 @@
 ITERS = 2
 STEP = 0.5
 GROUP = 16
+HALVES = 2
 F32, BF16 = jnp.float32, jnp.bfloat16
 
 
@@ -27,7 +28,7 @@
     n_flow, n_link,
     tiles_hbm, count_ref, flow_smem, flow_hbm, link_hbm, class_hbm, table_hbm, access_hbm, cap_hbm, price_hbm,
     rate_out, price_out,
-    tiles, flow_all, link_all, route_buf, load_buf, picked, term, rate_b, match, parts, own_class, own_access, price,
+    tiles, flow_all, link_all, route_buf, load_buf, picked, term, rate_b, match, spread, parts, own_class, own_access, price,
     flow_ref, link_ref, class_ref, table_ref, access_ref, cap_ref,
     tile_sem, in_sem, idx_send, flow_recv, link_recv, route_send, route_recv, load_send, load_recv,
 ):
@@ -88,6 +89,12 @@
             for k, peer in enumerate(flow_peers)
         ]
 
+    def copy_of(buf, index, send, recv, k, target, axis):
+        return pltpu.make_async_remote_copy(
+            src_ref=buf.at[index], dst_ref=buf.at[index], send_sem=send.at[k], recv_sem=recv.at[index],
+            device_id={axis: target}, device_id_type=pl.DeviceIdType.MESH,
+        )
+
     def arrived(buf, send, recv, k, source, axis):
         pltpu.make_async_remote_copy(
             src_ref=buf.at[source], dst_ref=buf.at[source], send_sem=send.at[k], recv_sem=recv.at[source],
@@ -95,6 +102,10 @@
         ).wait_recv()
 
     link_sources = [lax.rem(me_l + n_link - k, n_link) for k in range(1, n_link)]
+    partner = me_l + 1 - 2 * lax.rem(me_l, 2)
+    steps = sorted(range(1, n_link // 2), key=lambda k: min(k, n_link // 2 - k))
+    line = [lax.rem(me_l + 2 * k, n_link) for k in steps]
+    partner_line = [lax.rem(partner + 2 * k, n_link) for k in steps]
     flow_sources = [lax.rem(me_f + n_flow - k, n_flow) for k in range(1, n_flow)]
     pending = to_link(flow_all, idx_send.at[0], flow_recv) + to_flow(link_all, idx_send.at[1], link_recv)
     for copy in pending:
@@ -111,7 +122,7 @@
     row_used = iota((slots, size), 0) < count
     group_row = iota((GROUP, size), 0)
 
-    def route_terms(first):
+    def route_terms(first, half):
         def body(g, carry):
             at = pl.multiple_of(g * GROUP, GROUP)
             p = picked[pl.ds(at, GROUP), :]
@@ -122,15 +133,13 @@
             term[pl.ds(at, GROUP), :] = jnp.dot(left, right, preferred_element_type=F32)
             return carry
 
+        per = slots // HALVES // GROUP
         if first:
-            per = chunk // GROUP
-            for c, copy in enumerate(loads):
+            for copy in loads[half * len(loads) // HALVES : (half + 1) * len(loads) // HALVES]:
                 copy.wait()
-                lax.fori_loop(c * per, (c + 1) * per, body, 0)
-        else:
-            lax.fori_loop(0, slots // GROUP, body, 0)
-
-    def load_terms():
+        lax.fori_loop(half * per, (half + 1) * per, body, 0)
+
+    def load_terms(half):
         def body(g, carry):
             at = pl.multiple_of(g * GROUP, GROUP)
             q = rate_b[pl.ds(at, GROUP), :]
@@ -142,20 +151,27 @@
             term[pl.ds(at, GROUP), :] = total
             return carry
 
-        lax.fori_loop(0, slots // GROUP, body, 0)
-
-    def encode(buf, it, slot):
-        x = jnp.where(row_used, term[...], 0.0)
+        per = slots // HALVES // GROUP
+        lax.fori_loop(half * per, (half + 1) * per, body, 0)
+
+    part = slots // HALVES
+
+    def encode(buf, it, half, slot):
+        at = half * part
+        x = jnp.where(row_used[at : at + part], term[at : at + part, :], 0.0)
         level = jnp.ceil(jnp.log2(jnp.maximum(jnp.max(x, axis=0, keepdims=True), 1e-30)) * 8.0)
         y = jnp.sqrt(x * jnp.exp2(level * -0.125)) * 65535.0 - 32768.0
         code = jnp.clip(jnp.round(y), -32768.0, 32767.0).astype(jnp.int32)
-        buf[it, slot, :slots, :] = code.astype(jnp.int16)
-        buf[it, slot, slots:, :] = jnp.broadcast_to(level.astype(jnp.int32), (GROUP, size)).astype(jnp.int16)
+        buf[it, half, slot, :part, :] = code.astype(jnp.int16)
+        buf[it, half, slot, part:, :] = jnp.broadcast_to(level.astype(jnp.int32), (GROUP, size)).astype(jnp.int16)
 
     def decode(buf, it, slot):
-        y = (buf[it, slot, :slots, :].astype(jnp.int32).astype(F32) + 32768.0) * (1.0 / 65535.0)
-        level = buf[it, slot, slots:, :].astype(jnp.int32).astype(F32)[:1, :]
-        return y * y * jnp.exp2(level * 0.125)
+        found = []
+        for half in range(HALVES):
+            y = (buf[it, half, slot, :part, :].astype(jnp.int32).astype(F32) + 32768.0) * (1.0 / 65535.0)
+            level = buf[it, half, slot, part:, :].astype(jnp.int32).astype(F32)[:1, :]
+            found.append(y * y * jnp.exp2(level * 0.125))
+        return jnp.concatenate(found, axis=0)
 
     def weights(classes):
         out = jnp.zeros(classes.shape, F32)
@@ -168,12 +184,13 @@
     inputs[2].wait()
     for it in range(ITERS):
         picked[...] = jnp.dot(pick, price[...].astype(BF16), preferred_element_type=F32)
-        route_terms(it == 0)
-        encode(route_buf, it, me_l)
-        sends = to_link(route_buf.at[it], route_send.at[it], route_recv.at[it])
-        for copy in sends:
-            copy.start()
-        pending += sends
+        for half in range(HALVES):
+            route_terms(it == 0, half)
+            encode(route_buf, it, half, me_l)
+            for k, peer in enumerate(line + [partner]):
+                copy = copy_of(route_buf.at[it, half], me_l, route_send.at[it, half], route_recv.at[it, half], k, peer, "link")
+                copy.start()
+                pending.append(copy)
         if it == 0:
             for copy in inputs[3:]:
                 copy.wait()
@@ -195,24 +212,50 @@
                 match[d, :, slots:] = same
 
         route = jnp.zeros((slots, size), F32)
-        for k, source in enumerate([me_l] + link_sources):
-            if k:
-                arrived(route_buf.at[it], route_send.at[it], route_recv.at[it], k - 1, source, "link")
+        def add(source, route):
             high, low = halves(decode(route_buf, it, source))
             both = jnp.concatenate([high, low], axis=0)
             if it == ITERS - 1:
                 parts[source] = both
-            route = route + jnp.dot(match[source], both, preferred_element_type=F32)
+            return route + jnp.dot(match[source], both, preferred_element_type=F32)
+
+        def await_route(half, source):
+            copy_of(
+                route_buf.at[it, half], source, route_send.at[it, half], route_recv.at[it, half], 0, partner, "link"
+            ).wait_recv()
+
+        route = add(me_l, route)
+        for half in range(HALVES):
+            for k, source in enumerate(line):
+                await_route(half, source)
+                copy = copy_of(
+                    route_buf.at[it, half], source, route_send.at[it, half], route_recv.at[it, half],
+                    n_link // 2 + k, partner, "link",
+                )
+                copy.start()
+                pending.append(copy)
+        for source in line:
+            route = add(source, route)
+        for source in [partner] + partner_line:
+            for half in range(HALVES):
+                await_route(half, source)
+            route = add(source, route)
         rate_b[...] = (own_weight / (own_access[...] + route)).astype(BF16)
-        load_terms()
-        encode(load_buf, it, me_f)
-        sends = to_flow(load_buf.at[it], load_send.at[it], load_recv.at[it])
-        for copy in sends:
-            copy.start()
-        pending += sends
+        for half in range(HALVES):
+            load_terms(half)
+            encode(load_buf, it, half, me_f)
+            for k, peer in enumerate(flow_peers):
+                copy = copy_of(load_buf.at[it, half], me_f, load_send.at[it, half], load_recv.at[it, half], k, peer, "flow")
+                copy.start()
+                pending.append(copy)
         if it == 0:
             for k, source in enumerate(flow_sources):
                 arrived(link_all, idx_send.at[1], link_recv, k, source, "flow")
+            block_row = iota((link_blocks, slots), 0)
+            for d in range(n_flow):
+                same = (block_row == link_all[d, 0:1, :]).astype(F32).astype(BF16)
+                spread[d, :, :slots] = same
+                spread[d, :, slots:] = same
         if it == ITERS - 1:
             def rows(r, carry):
                 at = pl.multiple_of(r * size, size)
@@ -230,16 +273,15 @@
             lax.fori_loop(0, flow_blocks // size, rows, 0)
 
         load = jnp.zeros((link_blocks, size), F32)
-        block_row = iota((link_blocks, slots), 0)
         for k, source in enumerate([me_f] + flow_sources):
             if k:
-                arrived(load_buf.at[it], load_send.at[it], load_recv.at[it], k - 1, source, "flow")
+                for half in range(HALVES):
+                    copy_of(
+                        load_buf.at[it, half], source, load_send.at[it, half], load_recv.at[it, half], 0, source, "flow"
+                    ).wait_recv()
             high, low = halves(decode(load_buf, it, source))
-            same = (block_row == link_all[source, 0:1, :]).astype(F32).astype(BF16)
             load = load + jnp.dot(
-                jnp.concatenate([same, same], axis=1),
-                jnp.concatenate([high, low], axis=0),
-                preferred_element_type=F32,
+                spread[source], jnp.concatenate([high, low], axis=0), preferred_element_type=F32
             )
         new = price[...] * jnp.exp(STEP * (load / cap_ref[...] - 1.0))
         if it == ITERS - 1:
@@ -271,12 +313,13 @@
             pltpu.VMEM((slots, size, size), BF16),
             pltpu.VMEM((n_link, 8, slots), jnp.int32),
             pltpu.VMEM((n_flow, 8, slots), jnp.int32),
-            pltpu.VMEM((ITERS, n_link, slots + GROUP, size), jnp.int16),
-            pltpu.VMEM((ITERS, n_flow, slots + GROUP, size), jnp.int16),
+            pltpu.VMEM((ITERS, HALVES, n_link, slots // HALVES + GROUP, size), jnp.int16),
+            pltpu.VMEM((ITERS, HALVES, n_flow, slots // HALVES + GROUP, size), jnp.int16),
             pltpu.VMEM((slots, size), F32),
             pltpu.VMEM((slots, size), F32),
             pltpu.VMEM((slots, size), BF16),
             pltpu.VMEM((n_link, slots, 2 * slots), BF16),
+            pltpu.VMEM((n_flow, link_blocks, 2 * slots), BF16),
             pltpu.VMEM((n_link, 2 * slots, size), BF16),
             pltpu.VMEM((slots, size), jnp.int32),
             pltpu.VMEM((slots, size), F32),
@@ -292,10 +335,10 @@
             dma((2, peers)),
             dma((n_link,)),
             dma((n_flow,)),
-            dma((ITERS, n_link)),
-            dma((ITERS, n_link)),
-            dma((ITERS, n_flow)),
-            dma((ITERS, n_flow)),
+            dma((ITERS, HALVES, n_link)),
+            dma((ITERS, HALVES, n_link)),
+            dma((ITERS, HALVES, n_flow)),
+            dma((ITERS, HALVES, n_flow)),
         ],
         compiler_params=pltpu.CompilerParams(
             collective_id=0, has_side_effects=True, vmem_limit_bytes=60 * 1024 * 1024

time: 44.5 us -> 44.5 us (level)
  no operation moved by 1% of the time
where the time goes in v3:
time: 44.5 us; the launch traced here: 44.3 us
  Pallas kernels  39.5 us (89%)
  local copies, waits for them, and re-layouts  3.54 us (8%)
  between operations  1.29 us (3%)
    pallas_call x1, Pallas kernels, on_device(): pl.pallas_call(functools.partial(kernel, n_flow, n_link), out_shape=(jax....  39.5 us
    unnamed x2, local copies, waits for them, and re-layouts  3.54 us

profile of v3, /device:TPU:0, one launch (start us, length us, event | category | flops | bytes accessed | tf_op | source)
XLA Modules:
  0.0 44.3 jit_solution(10546186544729383467)
XLA Ops:
  1.3 39.5 %shard_map.104 = (f32[1024,128]{1,0:T(8,128)}, f32[512,128]{1,0:T(8,128)}) custom-call(bf16[128,128,128]{2,1,0:T(8,128)(2,1)} %tiles_hbm.1, s32[1,1]{1,0:T(1,128)S(6)} %copy.13.count_ref, s32[1,128]{1,0:T(1,128)} %flow_hbm.1, s32[1,128]{1,0:T(1,128)} %flow_hbm.1, s32[1,128]{1,0:T(1,128)} %link_hbm.1, s32[1024,128]{1,0:T(8,128)} %bitcast.7, ...), custom_call_target="tpu_custom_call" | custom-call | tf_op jit(solution)/shard_map/pallas_call | solution.py:304
  40.7 1.9 %copy.14 = f32[131072]{0:T(1024)} copy(f32[131072]{0:T(1024)} %bitcast.9) | data formatting | bytes 1048576
  42.6 1.7 %copy.15 = f32[65536]{0:T(1024)} copy(f32[65536]{0:T(1024)} %bitcast.12) | data formatting | bytes 524288

commit v4 on v3

--- a/solution.py
+++ b/solution.py
@@ -10,7 +10,7 @@
 ITERS = 2
 STEP = 0.5
 GROUP = 16
-HALVES = 2
+HALVES = 1
 F32, BF16 = jnp.float32, jnp.bfloat16
 
 
@@ -30,15 +30,18 @@
     rate_out, price_out,
     tiles, flow_all, link_all, route_buf, load_buf, picked, term, rate_b, match, spread, parts, own_class, own_access, price,
     flow_ref, link_ref, class_ref, table_ref, access_ref, cap_ref,
-    tile_sem, in_sem, idx_send, flow_recv, link_recv, route_send, route_recv, load_send, load_recv,
+    tile_sem, in_sem, route_send, route_recv, load_send, load_recv,
 ):
     slots, size = tiles.shape[0], tiles.shape[1]
     link_blocks, flow_blocks = price.shape[0], access_ref.shape[0]
     me_f, me_l = lax.axis_index("flow"), lax.axis_index("link")
     barrier = pltpu.get_barrier_semaphore()
-    link_peers = [lax.rem(me_l + k, n_link) for k in range(1, n_link)]
+    partner = me_l + 1 - 2 * lax.rem(me_l, 2)
+    steps = sorted(range(1, n_link // 2), key=lambda k: min(k, n_link // 2 - k))
+    line = [lax.rem(me_l + 2 * k, n_link) for k in steps]
+    partner_line = [lax.rem(partner + 2 * k, n_link) for k in steps]
     flow_peers = [lax.rem(me_f + k, n_flow) for k in range(1, n_flow)]
-    for peer in link_peers:
+    for peer in line + [partner]:
         pl.semaphore_signal(barrier, inc=1, device_id={"link": peer})
     for peer in flow_peers:
         pl.semaphore_signal(barrier, inc=1, device_id={"flow": peer})
@@ -69,25 +72,6 @@
     used = iota((8, slots), 1) < count
     flow_all[me_l] = jnp.where(used, jnp.broadcast_to(flow_ref[...], (8, slots)), -1)
     link_all[me_f] = jnp.where(used, jnp.broadcast_to(link_ref[...], (8, slots)), -1)
-    pl.semaphore_wait(barrier, n_link + n_flow - 2)
-
-    def to_link(buf, send, recv):
-        return [
-            pltpu.make_async_remote_copy(
-                src_ref=buf.at[me_l], dst_ref=buf.at[me_l], send_sem=send.at[k], recv_sem=recv.at[me_l],
-                device_id={"link": peer}, device_id_type=pl.DeviceIdType.MESH,
-            )
-            for k, peer in enumerate(link_peers)
-        ]
-
-    def to_flow(buf, send, recv):
-        return [
-            pltpu.make_async_remote_copy(
-                src_ref=buf.at[me_f], dst_ref=buf.at[me_f], send_sem=send.at[k], recv_sem=recv.at[me_f],
-                device_id={"flow": peer}, device_id_type=pl.DeviceIdType.MESH,
-            )
-            for k, peer in enumerate(flow_peers)
-        ]
 
     def copy_of(buf, index, send, recv, k, target, axis):
         return pltpu.make_async_remote_copy(
@@ -95,21 +79,8 @@
             device_id={axis: target}, device_id_type=pl.DeviceIdType.MESH,
         )
 
-    def arrived(buf, send, recv, k, source, axis):
-        pltpu.make_async_remote_copy(
-            src_ref=buf.at[source], dst_ref=buf.at[source], send_sem=send.at[k], recv_sem=recv.at[source],
-            device_id={axis: source}, device_id_type=pl.DeviceIdType.MESH,
-        ).wait_recv()
-
-    link_sources = [lax.rem(me_l + n_link - k, n_link) for k in range(1, n_link)]
-    partner = me_l + 1 - 2 * lax.rem(me_l, 2)
-    steps = sorted(range(1, n_link // 2), key=lambda k: min(k, n_link // 2 - k))
-    line = [lax.rem(me_l + 2 * k, n_link) for k in steps]
-    partner_line = [lax.rem(partner + 2 * k, n_link) for k in steps]
     flow_sources = [lax.rem(me_f + n_flow - k, n_flow) for k in range(1, n_flow)]
-    pending = to_link(flow_all, idx_send.at[0], flow_recv) + to_flow(link_all, idx_send.at[1], link_recv)
-    for copy in pending:
-        copy.start()
+    pending = []
 
     def column(row):
         return jnp.broadcast_to(row.astype(F32), (slots, slots)).T
@@ -156,14 +127,16 @@
 
     part = slots // HALVES
 
-    def encode(buf, it, half, slot):
+    def encode(buf, it, half, slot, numbers):
         at = half * part
         x = jnp.where(row_used[at : at + part], term[at : at + part, :], 0.0)
         level = jnp.ceil(jnp.log2(jnp.maximum(jnp.max(x, axis=0, keepdims=True), 1e-30)) * 8.0)
         y = jnp.sqrt(x * jnp.exp2(level * -0.125)) * 65535.0 - 32768.0
         code = jnp.clip(jnp.round(y), -32768.0, 32767.0).astype(jnp.int32)
         buf[it, half, slot, :part, :] = code.astype(jnp.int16)
-        buf[it, half, slot, part:, :] = jnp.broadcast_to(level.astype(jnp.int32), (GROUP, size)).astype(jnp.int16)
+        buf[it, half, slot, part:, :] = jnp.where(
+            group_row < GROUP // 2, level.astype(jnp.int32), numbers[slot, 0:1, :]
+        ).astype(jnp.int16)
 
     def decode(buf, it, slot):
         found = []
@@ -173,6 +146,10 @@
             found.append(y * y * jnp.exp2(level * 0.125))
         return jnp.concatenate(found, axis=0)
 
+    def numbers_of(buf, it, slot):
+        row = buf[it, 0, slot, part:, :].astype(jnp.int32)[GROUP // 2 :, :]
+        return row[:8, :]
+
     def weights(classes):
         out = jnp.zeros(classes.shape, F32)
         low, high = classes % size, classes // size
@@ -186,7 +163,9 @@
         picked[...] = jnp.dot(pick, price[...].astype(BF16), preferred_element_type=F32)
         for half in range(HALVES):
             route_terms(it == 0, half)
-            encode(route_buf, it, half, me_l)
+            encode(route_buf, it, half, me_l, flow_all)
+            if it == 0 and half == 0:
+                pl.semaphore_wait(barrier, n_link // 2 + n_flow - 1)
             for k, peer in enumerate(line + [partner]):
                 copy = copy_of(route_buf.at[it, half], me_l, route_send.at[it, half], route_recv.at[it, half], k, peer, "link")
                 copy.start()
@@ -203,16 +182,17 @@
 
             lax.fori_loop(0, slots, own, 0, unroll=8)
             own_weight = weights(own_class[...])
-            for k, source in enumerate(link_sources):
-                arrived(flow_all, idx_send.at[0], flow_recv, k, source, "link")
             flow_col = column(flow_ref[...])
-            for d in range(n_link):
-                same = (flow_col == flow_all[d, 0:1, :].astype(F32)).astype(BF16)
-                match[d, :, :slots] = same
-                match[d, :, slots:] = same
 
         route = jnp.zeros((slots, size), F32)
+
         def add(source, route):
+            if it == 0:
+                row = numbers_of(route_buf, it, source)
+                flow_all[source] = row
+                same = (flow_col == row[0:1, :].astype(F32)).astype(BF16)
+                match[source, :, :slots] = same
+                match[source, :, slots:] = same
             high, low = halves(decode(route_buf, it, source))
             both = jnp.concatenate([high, low], axis=0)
             if it == ITERS - 1:
@@ -243,19 +223,11 @@
         rate_b[...] = (own_weight / (own_access[...] + route)).astype(BF16)
         for half in range(HALVES):
             load_terms(half)
-            encode(load_buf, it, half, me_f)
+            encode(load_buf, it, half, me_f, link_all)
             for k, peer in enumerate(flow_peers):
                 copy = copy_of(load_buf.at[it, half], me_f, load_send.at[it, half], load_recv.at[it, half], k, peer, "flow")
                 copy.start()
                 pending.append(copy)
-        if it == 0:
-            for k, source in enumerate(flow_sources):
-                arrived(link_all, idx_send.at[1], link_recv, k, source, "flow")
-            block_row = iota((link_blocks, slots), 0)
-            for d in range(n_flow):
-                same = (block_row == link_all[d, 0:1, :]).astype(F32).astype(BF16)
-                spread[d, :, :slots] = same
-                spread[d, :, slots:] = same
         if it == ITERS - 1:
             def rows(r, carry):
                 at = pl.multiple_of(r * size, size)
@@ -279,6 +251,11 @@
                     copy_of(
                         load_buf.at[it, half], source, load_send.at[it, half], load_recv.at[it, half], 0, source, "flow"
                     ).wait_recv()
+            if it == 0:
+                row = numbers_of(load_buf, it, source)
+                same = (iota((link_blocks, slots), 0) == row[0:1, :]).astype(F32).astype(BF16)
+                spread[source, :, :slots] = same
+                spread[source, :, slots:] = same
             high, low = halves(decode(load_buf, it, source))
             load = load + jnp.dot(
                 spread[source], jnp.concatenate([high, low], axis=0), preferred_element_type=F32
@@ -300,7 +277,6 @@
     hbm = pl.BlockSpec(memory_space=pltpu.HBM)
     smem = pl.BlockSpec(memory_space=pltpu.SMEM)
     dma = pltpu.SemaphoreType.DMA
-    peers = max(n_flow, n_link)
     rate, price = pl.pallas_call(
         functools.partial(kernel, n_flow, n_link),
         out_shape=(
@@ -332,9 +308,6 @@
             pltpu.VMEM((link_blocks, size), F32),
             dma((4,)),
             dma((7,)),
-            dma((2, peers)),
-            dma((n_link,)),
-            dma((n_flow,)),
             dma((ITERS, HALVES, n_link)),
             dma((ITERS, HALVES, n_link)),
             dma((ITERS, HALVES, n_flow)),

time: 44.5 us -> 44 us (0.989)
  Pallas kernels: 39.5 us -> 39 us
where the time goes in v4:
time: 44 us; the launch traced here: 43.8 us
  Pallas kernels  39 us (89%)
  local copies, waits for them, and re-layouts  3.54 us (8%)
  between operations  1.29 us (3%)
    pallas_call x1, Pallas kernels, on_device(): pl.pallas_call(functools.partial(kernel, n_flow, n_link), out_shape=(jax....  39 us
    unnamed x2, local copies, waits for them, and re-layouts  3.54 us

profile of v4, /device:TPU:0, one launch (start us, length us, event | category | flops | bytes accessed | tf_op | source)
XLA Modules:
  0.0 43.8 jit_solution(12088624397322195736)
XLA Ops:
  1.3 39.0 %shard_map.104 = (f32[1024,128]{1,0:T(8,128)}, f32[512,128]{1,0:T(8,128)}) custom-call(bf16[128,128,128]{2,1,0:T(8,128)(2,1)} %tiles_hbm.1, s32[1,1]{1,0:T(1,128)S(6)} %copy.13.count_ref, s32[1,128]{1,0:T(1,128)} %flow_hbm.1, s32[1,128]{1,0:T(1,128)} %flow_hbm.1, s32[1,128]{1,0:T(1,128)} %link_hbm.1, s32[1024,128]{1,0:T(8,128)} %bitcast.7, ...), custom_call_target="tpu_custom_call" | custom-call | tf_op jit(solution)/shard_map/pallas_call | solution.py:280
  40.3 1.9 %copy.14 = f32[131072]{0:T(1024)} copy(f32[131072]{0:T(1024)} %bitcast.9) | data formatting | bytes 1048576
  42.2 1.7 %copy.15 = f32[65536]{0:T(1024)} copy(f32[65536]{0:T(1024)} %bitcast.12) | data formatting | bytes 524288

commit v5 on v4

--- a/solution.py
+++ b/solution.py
@@ -10,7 +10,7 @@
 ITERS = 2
 STEP = 0.5
 GROUP = 16
-HALVES = 1
+HALVES = 2
 F32, BF16 = jnp.float32, jnp.bfloat16
 
 
@@ -267,6 +267,25 @@
             price[...] = new
     for copy in pending:
         copy.wait_send()
+
+
+def move(rate, price, rate_out, price_out, rate_held, price_held, sem):
+    copies = []
+    for source, held, target in ((rate, rate_held, rate_out), (price, price_held, price_out)):
+        rows = source.shape[0] // 2
+        for c in range(2):
+            block, k = pl.ds(c * rows, rows), len(copies)
+            copies.append((
+                pltpu.make_async_copy(source.at[block], held.at[block], sem.at[0, k]),
+                pltpu.make_async_copy(held.at[block], target.at[block], sem.at[1, k]),
+            ))
+    for first, _ in copies:
+        first.start()
+    for first, second in copies:
+        first.wait()
+        second.start()
+    for _, second in copies:
+        second.wait()
 
 
 def on_device(n_flow, n_link, route_tiles, tile_count, tile_flow, tile_link, flow_class, class_weight, access_price,
@@ -322,6 +341,19 @@
         access_price.reshape(flow_blocks, size), capacity.reshape(link_blocks, size),
         init_price.reshape(link_blocks, size),
     )
+    rate, price = pl.pallas_call(
+        move,
+        out_shape=(
+            jax.ShapeDtypeStruct((flow_blocks, size), F32),
+            jax.ShapeDtypeStruct((link_blocks, size), F32),
+        ),
+        in_specs=[hbm, hbm],
+        out_specs=(hbm, hbm),
+        scratch_shapes=[
+            pltpu.VMEM((flow_blocks, size), F32), pltpu.VMEM((link_blocks, size), F32), dma((2, 4)),
+        ],
+        compiler_params=pltpu.CompilerParams(vmem_limit_bytes=60 * 1024 * 1024),
+    )(rate, price)
     return rate.reshape(-1), price.reshape(-1)
 
 

time: 44 us -> 40.9 us (0.930)
  local copies, waits for them, and re-layouts: 3.54 us -> 0 us
    unnamed x2 -> x0, local copies, waits for them, and re-layouts: 3.54 us -> none
    pallas_call x0 -> x1, Pallas kernels: none -> 1.89 us  [on_device(): pl.pallas_call(move, out_shape=(jax.ShapeDtypeStruct((flow_blocks, size),...]
    pallas_call x1, Pallas kernels: 39 us -> 37.5 us  [on_device(): pl.pallas_call(functools.partial(kernel, n_flow, n_link), out_shape=(jax....]
where the time goes in v5:
time: 40.9 us; the launch traced here: 40.7 us
  Pallas kernels  39.4 us (96%)
  between operations  1.29 us (3%)
    pallas_call x1, Pallas kernels, on_device(): pl.pallas_call(functools.partial(kernel, n_flow, n_link), out_shape=(jax....  37.5 us
    pallas_call x1, Pallas kernels, on_device(): pl.pallas_call(move, out_shape=(jax.ShapeDtypeStruct((flow_blocks, size),...  1.89 us

profile of v5, /device:TPU:0, one launch (start us, length us, event | category | flops | bytes accessed | tf_op | source)
XLA Modules:
  0.0 40.7 jit_solution(16307831654924153901)
XLA Ops:
  1.3 37.5 %shard_map.104 = (f32[1024,128]{1,0:T(8,128)}, f32[512,128]{1,0:T(8,128)}) custom-call(bf16[128,128,128]{2,1,0:T(8,128)(2,1)} %tiles_hbm.1, s32[1,1]{1,0:T(1,128)S(6)} %copy.11.count_ref, s32[1,128]{1,0:T(1,128)} %flow_hbm.1, s32[1,128]{1,0:T(1,128)} %flow_hbm.1, s32[1,128]{1,0:T(1,128)} %link_hbm.1, s32[1024,128]{1,0:T(8,128)} %bitcast.7, ...), custom_call_target="tpu_custom_call" | custom-call | tf_op jit(solution)/shard_map/pallas_call | solution.py:299
  38.8 1.9 %shard_map.105 = (f32[1024,128]{1,0:T(8,128)}, f32[512,128]{1,0:T(8,128)}) custom-call(f32[1024,128]{1,0:T(8,128)} %get-tuple-element.6.rate, f32[512,128]{1,0:T(8,128)} %get-tuple-element.7.price), custom_call_target="tpu_custom_call" | custom-call | tf_op jit(solution)/shard_map/pallas_call | solution.py:344
